TPU v7x, 768 devices: a whole 4x8x12 slice. The times are simulated.
768 devices in a mesh: row: 96 (over y, z_lo, x), col: 8 (over z_hi, core).
Axes of the slice: x: 4, y: 8, z: 12 (z_hi: 4, z_lo: 3; z = z_hi * 3 + z_lo), core: 2. Of those that a mesh axis runs over, the one named last changes fastest.
Arguments:
- features: bfloat16 [98304, 256], P(('row', 'col')), may hold values from -6 to 6
- weight: float32 [256, 256], replicated, may hold values from -0.375 to 0.375
- bias: float32 [256], replicated, may hold values from -3 to 3
- cotangent: bfloat16 [98304, 256], P(('row', 'col')), may hold values from -6 to 6
- tile_values: bfloat16 [96, 8, 24, 128, 128], P('row', 'col'), may hold values from -0.3125 to 0.3125
- tile_pos: int32 [96, 8, 24], P('row', 'col'), may hold values from 0 to 767, as said below
- tile_count: int32 [96, 8], P('row', 'col'), may hold values from 1 to 24, as said below
Outputs:
- output: bfloat16 [98304, 256], P(('row', 'col'))
- grad_weight: float32 [256, 256], replicated
- grad_bias: float32 [256], replicated
- grad_input: bfloat16 [98304, 256], P(('row', 'col'))
Inputs may be any that keep to these rules, and one draw needn't show every extreme that they name: `tile_pos`: the 24 positions of one device are distinct; some device holds positions 0 and 767. `tile_count`: some device uses all 24 slots.
All inputs are finite; a program needn't handle non-finite values.
Results may differ from a plain program's by a relative error of at most 0.008.
Values may be sent and summed in bfloat16 or wider, within the bound.
A program may use at most 64 MiB of HBM per device.

v0:
```python
import math

import jax
import jax.numpy as jnp
from jax import lax
from jax.sharding import PartitionSpec as P

TILE = 128


def silu_slope(values):
    sig = jax.nn.sigmoid(values)
    return sig * (1.0 + values * (1.0 - sig))


def per_device(features, weight, bias, cotangent, tile_values, tile_pos, tile_count):
    node_rows, feat_dim = features.shape
    row_devs = lax.axis_size("row")
    col_devs = lax.axis_size("col")
    col_tiles = node_rows * row_devs // TILE
    row_tiles = node_rows * col_devs // TILE
    values = tile_values[0, 0]
    places = tile_pos[0, 0]
    in_use = tile_count[0, 0]
    slot_total = values.shape[0]
    active = jnp.arange(slot_total) < in_use
    row_of = places // col_tiles
    col_of = places % col_tiles
    gathered = lax.all_gather(features, "row", axis=0, tiled=True).reshape(
        col_tiles, TILE, feat_dim
    )
    product = jnp.einsum(
        "kij,kjf->kif", values, gathered[col_of], preferred_element_type=jnp.float32
    )
    product = jnp.where(active[:, None, None], product, 0.0)
    partial_value = jnp.zeros((row_tiles, TILE, feat_dim), jnp.float32).at[row_of].add(product)
    partial_value = partial_value.reshape(row_tiles * TILE, feat_dim)
    hidden = lax.psum_scatter(partial_value, "col", scatter_dimension=0, tiled=True)
    pre_act = jnp.dot(hidden, weight, precision=lax.Precision.HIGHEST) + bias
    grad_pre = (cotangent.astype(jnp.float32) * silu_slope(pre_act)).astype(jnp.bfloat16)
    block_dpre = lax.all_gather(grad_pre, "col", axis=0, tiled=True)
    output = jax.nn.silu(pre_act).astype(jnp.bfloat16)
    factor = 1.0 / math.sqrt(node_rows * row_devs * col_devs)
    grad_float = grad_pre.astype(jnp.float32)
    local_weight = jnp.dot(hidden.T, grad_float, precision=lax.Precision.HIGHEST) * factor
    local_bias = jnp.sum(grad_float, axis=0) * factor
    grad_weight, grad_bias = lax.psum((local_weight, local_bias), ("row", "col"))
    grad_rows = block_dpre.reshape(row_tiles, TILE, feat_dim)
    product_back = jnp.einsum(
        "kij,kif->kjf", values, grad_rows[row_of], preferred_element_type=jnp.float32
    )
    product_back = jnp.where(active[:, None, None], product_back, 0.0)
    backward = jnp.zeros((col_tiles, TILE, feat_dim), jnp.float32).at[col_of].add(product_back)
    backward = backward.reshape(col_tiles * TILE, feat_dim)
    adjoint = lax.psum_scatter(backward, "row", scatter_dimension=0, tiled=True)
    grad_input = jnp.dot(adjoint, weight.T, precision=lax.Precision.HIGHEST).astype(jnp.bfloat16)
    return (output, grad_weight, grad_bias, grad_input)


def solution(mesh):
    in_specs = (
        P(("row", "col"), None),
        P(),
        P(),
        P(("row", "col"), None),
        P("row", "col", None, None, None),
        P("row", "col", None),
        P("row", "col"),
    )
    out_specs = (P(("row", "col"), None), P(), P(), P(("row", "col"), None))
    return jax.shard_map(
        per_device, mesh=mesh, in_specs=in_specs, out_specs=out_specs, check_vma=False
    )
```

profile of v0, /device:TPU:1, one launch (start us, length us, event | category | flops | bytes accessed | tf_op | source)
XLA Modules:
  0.0 1739.5 jit_solution(5905221999645679570)
XLA Ops:
  7.2 0.0 copy-start
  7.2 0.0 all-gather.2.cloned.1.call-start
  7.2 0.7 all-gather.2.cloned.1.call-update
  7.9 0.0 reduce-scatter.3.cloned.1.call-start
  8.6 0.7 fusion.4
  9.3 441.5 %all-gather.2.cloned.1.call-done = bf16[12288,256]{1,0:T(8,128)(2,1)} async-done(((bf16[128,256]{1,0:T(8,128)(2,1)}), bf16[12288,256]{1,0:T(8,128)(2,1)}) %all-gather.2.cloned.1.call-update) | async-done | bytes 6291472 | tf_op jit(solution)/shard_map/all_gather | solution.py:29
  450.8 3.4 gather_fusion
  454.3 0.0 copy-done
  454.3 2.4 select_bitcast_fusion.1
  456.7 3.6 copy.14
  460.3 0.1 broadcast_in_dim.29
  460.3 0.0 copy-start.2
  460.4 0.0 copy-start.4
  460.4 0.0 copy-start.5
  460.4 6.1 scatter_fusion
  466.5 0.0 copy-start.1
  466.5 1.0 copy-done.1
  467.5 0.0 reduce-scatter.3.cloned.1.call-update
  467.5 0.0 reduce-scatter.5.cloned.1.call-start
  467.5 160.3 %reduce-scatter.3.cloned.1.call-done = f32[128,256]{1,0:T(8,128)} async-done(((f32[1024,256]{1,0:T(8,128)}), f32[128,256]{1,0:T(8,128)}) %reduce-scatter.3.cloned.1.call-update) | async-done | bytes 131088 | tf_op jit(solution)/shard_map/reduce_scatter | solution.py:38
  627.9 0.0 copy-done.2
  627.9 0.0 copy-done.4
  627.9 0.0 copy-done.5
  627.9 1.9 convert_reduce_fusion
  629.7 20.8 %all_gather.7 = bf16[1024,256]{1,0:T(8,128)(2,1)S(1)} all-gather(bf16[128,256]{1,0:T(8,128)(2,1)S(1)} %get-tuple-element.5), channel_id=1, replica_groups=mesh['row'=96,'col'=8] {'col'}, dimensions={0}, use_global_device_ids=true | all-gather | bytes 589824 | tf_op jit(solution)/shard_map/all_gather | solution.py:41
  650.5 0.6 gather_fusion.1
  651.1 2.4 select_bitcast_fusion
  653.5 3.6 copy.16
  657.1 6.1 broadcast_in_dim.32
  663.2 9.4 scatter_fusion.1
  672.7 0.0 copy-start.3
  672.7 0.0 reduce-scatter.5.cloned.1.call-update
  672.7 0.0 all-reduce.2.cloned.1.call-start
  672.7 109.2 %psum.15 = f32[256]{0:T(256)} all-reduce(f32[256]{0:T(256)S(1)} %broadcast_multiply_fusion), channel_id=1, replica_groups=mesh['row'=96,'col'=8] {'row','col'}, use_global_device_ids=true, to_apply=%region_4.5 | all-reduce | flops 256 | bytes 2048 | tf_op jit(solution)/shard_map/psum | solution.py:47
  782.0 0.0 copy-done.3
  782.0 1.0 convolution_multiply_fusion
  783.0 0.0 all-reduce.2.cloned.1.call-update
  783.0 356.5 %reduce-scatter.5.cloned.1.call-done = f32[128,256]{1,0:T(8,128)} async-done(((f32[12288,256]{1,0:T(8,128)}), f32[128,256]{1,0:T(8,128)}) %reduce-scatter.5.cloned.1.call-update) | async-done | bytes 131088 | tf_op jit(solution)/shard_map/reduce_scatter | solution.py:55
  1139.5 1.9 convolution_convert_fusion
  1141.5 589.9 %all-reduce.2.cloned.1.call-done = f32[256,256]{1,0:T(8,128)} async-done(((f32[256,256]{1,0:T(8,128)}), f32[256,256]{1,0:T(8,128)}) %all-reduce.2.cloned.1.call-update) | async-done | bytes 262160 | tf_op jit(solution)/shard_map/psum | solution.py:47
  1731.3 1.7 copy.23
  (4 shorter events, 0.0 us)
Async XLA Ops:
  7.2 447.1 %copy-start = (bf16[1,1,24,128,128]{4,3,2,1,0:T(8,128)(2,1)S(1)}, bf16[1,1,24,128,128]{4,3,2,1,0:T(8,128)(2,1)}, u32[]{:S(2)}) copy-start(bf16[1,1,24,128,128]{4,3,2,1,0:T(8,128)(2,1)} %param.11) | copy-start | bytes 2359300
  7.2 443.6 %all-gather.2.cloned.1.call-start = ((), (), s32[]{:S(2)}) async-start(), calls=%async_computation.2 | async-start | bytes 6356992 | tf_op jit(solution)/shard_map/all_gather | solution.py:29
  7.9 619.9 %reduce-scatter.3.cloned.1.call-start = ((), (), s32[]{:S(2)}) async-start(), calls=%async_computation.3 | async-start | bytes 1179648 | tf_op jit(solution)/shard_map/reduce_scatter | solution.py:38
  460.3 167.5 %copy-start.2 = (f32[256,256]{1,0:T(8,128)S(1)}, f32[256,256]{1,0:T(8,128)}, u32[]{:S(2)}) copy-start(f32[256,256]{1,0:T(8,128)} %param.8) | copy-start | bytes 786436
  460.4 167.5 %copy-start.4 = (bf16[128,256]{1,0:T(8,128)(2,1)S(1)}, bf16[128,256]{1,0:T(8,128)(2,1)}, u32[]{:S(2)}) copy-start(bf16[128,256]{1,0:T(8,128)(2,1)} %param.10) | copy-start | bytes 196612
  460.4 167.5 %copy-start.5 = (f32[256]{0:T(256)S(1)}, f32[256]{0:T(256)}, u32[]{:S(2)}) copy-start(f32[256]{0:T(256)} %param.9) | copy-start | bytes 3076
  466.5 1.0 copy-start.1
  467.5 672.0 %reduce-scatter.5.cloned.1.call-start = ((), (), s32[]{:S(2)}) async-start(), calls=%async_computation.5 | async-start | bytes 12713984 | tf_op jit(solution)/shard_map/reduce_scatter | solution.py:55
  672.7 109.3 %copy-start.3 = (f32[128,256]{1,0:T(8,128)S(1)}, f32[128,256]{1,0:T(8,128)}, u32[]{:S(2)}) copy-start(f32[128,256]{1,0:T(8,128)} %reduce-scatter.3.cloned.1.call-done) | copy-start | bytes 393220
  672.7 1058.7 %all-reduce.2.cloned.1.call-start = ((), (), s32[]{:S(2)}) async-start(), calls=%async_computation.4 | async-start | bytes 524288 | tf_op jit(solution)/shard_map/psum | solution.py:47
Sparse Core Ops, SparseCore 0:
  10.4 440.3 all-gather.1
  467.6 160.2 reduce-scatter.2
  672.8 466.6 reduce-scatter.4
  1145.4 585.9 all-reduce.1
where the time goes:
time: 1740 us
  waiting for transfers between devices  1550 us (89%)
  blocking collectives  130 us (7%)
  local copies, waits for them, and re-layouts  20.1 us (1%)
    psum x1, waiting for transfers between devices, per_device(): lax.psum((local_weight, local_bias), ('row', 'col'))  590 us
    all_gather x1, waiting for transfers between devices, per_device(): lax.all_gather(features, 'row', axis=0, tiled=True)  442 us
    reduce_scatter x1, waiting for transfers between devices, per_device(): adjoint = lax.psum_scatter(backward, 'row', scatter_dimension=0, tiled=True)  356 us
    reduce_scatter x1, waiting for transfers between devices, per_device(): lax.psum_scatter(partial_value, 'col', scatter_dimension=0, tiled=True)  160 us
    psum x1, blocking collectives, per_device(): lax.psum((local_weight, local_bias), ('row', 'col'))  109 us
  transfers between devices with their start and end apart: 4, of which 4 were waited for; matrix products, arithmetic and copies ran while one was open for 0% of the time, Pallas kernels for 0%

commit v1 on v0

v1 whole, which is shorter than its diff:
```python
import math

import jax
import jax.numpy as jnp
from jax import lax
from jax.experimental import pallas as pl
from jax.experimental.pallas import tpu as pltpu
from jax.sharding import PartitionSpec as P

TILE = 128
FEAT = 256
NY, NZ, NX = 8, 3, 4
NH, NC = 4, 2
SLOTS = 24
RT = NH * NC
CT = NY * NZ * NX
CUT = 48
MID = 96
NSEM = 160
MESH = pl.DeviceIdType.MESH
HIGHEST = lax.Precision.HIGHEST
F32 = jnp.float32
BF16 = jnp.bfloat16
FIRST = pl.ds(0, CUT)
SECOND = pl.ds(CUT, TILE - CUT)


def kernel(table, links, feat, weight, bias, cot, vals, out, gw, gb, gin,
           gath, flip, acc, part, hpart, hcore, hline, grow,
           ring_p, line_p, line_q, ring_q, zline,
           wbuf, wcore, wx, wy, wz, wh, wout, ssem, rsem):
    row = lax.axis_index("row")
    col = lax.axis_index("col")
    y, z, x = row // (NZ * NX), (row // NX) % NZ, row % NX
    h, c = col // NC, col % NC

    def at_x(s):
        return lax.rem(x + s + NX, NX)

    def at_y(s):
        return lax.rem(y + s + NY, NY)

    def at_z(s):
        return lax.rem(z + s, NZ)

    def at_h(s):
        return lax.rem(h + s + NH, NH)

    def to_x(s):
        return ((y * NZ + z) * NX + at_x(s), col)

    def to_y(s):
        return ((at_y(s) * NZ + z) * NX + x, col)

    def to_z(s):
        return ((y * NZ + at_z(s)) * NX + x, col)

    def to_h(index):
        return (row, index * NC + c)

    other_core = 1 - c
    partner = (row, h * NC + other_core)
    turn = 1 - 2 * c
    near = at_h(turn)
    back = at_h(-turn)
    far = at_h(2)

    copies = []

    def send(src, dst, target):
        index = len(copies)
        copy = pltpu.make_async_remote_copy(
            src_ref=src, dst_ref=dst, send_sem=ssem.at[index], recv_sem=rsem.at[index],
            device_id=target, device_id_type=MESH)
        copy.start()
        copies.append(copy)
        return copy

    barrier = pltpu.get_barrier_semaphore()
    friends = [to_x(s) for s in (1, 2, 3)] + [to_y(s) for s in range(1, NY)]
    friends += [to_z(s) for s in (1, 2)] + [to_h(at_h(s)) for s in (1, 2, 3)] + [partner]
    for friend in friends:
        pl.semaphore_signal(barrier, inc=1, device_id=friend, device_id_type=MESH)
    gath[y, z, x] = feat[...]
    pl.semaphore_wait(barrier, len(friends))

    zs = [send(feat, gath.at[y, z, x], to_z(s)) for s in (1, 2)]
    acc[SLOTS] = jnp.zeros((TILE, FEAT), F32)
    for k in range(SLOTS):
        flip[k] = vals[k].T
    for cp in zs:
        cp.wait_recv()

    def q_direct(s):
        block = gath.at[at_y(s), :, x, SECOND, :]
        return {1: send(block, block, to_x(1)), -1: send(block, block, to_x(-1))}

    def q_forward(s, arrived):
        way = 1 if s % 2 == 0 else -1
        arrived[way].wait_recv()
        block = gath.at[at_y(s), :, at_x(-way), SECOND, :]
        return [arrived[-way], send(block, block, to_x(way))]

    own_q = gath.at[y, :, x, SECOND, :]
    ring_up = send(own_q, own_q, to_y(1))
    ring_down = send(own_q, own_q, to_y(-1))
    own_p = gath.at[y, :, x, FIRST, :]
    px = [send(own_p, own_p, to_x(s)) for s in (1, 2, 3)]
    direct = {0: q_direct(0)}
    pending = []
    for cp in px:
        cp.wait_recv()
    block = gath.at[y, :, :, FIRST, :]
    p_up = send(block, block, to_y(1))
    p_down = send(block, block, to_y(-1))
    previous = [0]
    for s in (1, 2, 3, 4):
        ring_up.wait_recv()
        ring_down.wait_recv()
        if s < 3:
            block = gath.at[at_y(-s), :, x, SECOND, :]
            ring_up = send(block, block, to_y(1))
            block = gath.at[at_y(s), :, x, SECOND, :]
            ring_down = send(block, block, to_y(-1))
        elif s == 3:
            block = gath.at[at_y(-s), :, x, pl.ds(CUT, MID - CUT), :]
            ring_up = send(block, block, to_y(1))
            block = gath.at[at_y(s), :, x, pl.ds(MID, TILE - MID), :]
            ring_down = send(block, block, to_y(-1))
        current = [-s, s] if s < 4 else [4]
        for t in current:
            direct[t] = q_direct(t)
        for t in previous:
            pending += q_forward(t, direct[t])
        previous = current
        p_up.wait_recv()
        p_down.wait_recv()
        if s < 3:
            block = gath.at[at_y(-s), :, :, FIRST, :]
            p_up = send(block, block, to_y(1))
            block = gath.at[at_y(s), :, :, FIRST, :]
            p_down = send(block, block, to_y(-1))
        elif s == 3:
            block = gath.at[at_y(-s), :, 0:2, FIRST, :]
            p_up = send(block, block, to_y(1))
            block = gath.at[at_y(s), :, 2:4, FIRST, :]
            p_down = send(block, block, to_y(-1))
    for t in previous:
        pending += q_forward(t, direct[t])
    for cp in pending:
        cp.wait_recv()

    for k in range(SLOTS):
        spot = table[1, k]
        block = gath[spot // (NZ * NX), (spot // NX) % NZ, spot % NX]
        value = jnp.dot(vals[k], block, preferred_element_type=F32)
        acc[k] = value + acc[links[k]]
    for r in range(RT):
        hpart[r % NC, r // NC] = acc[links[SLOTS + r]].astype(BF16)

    cp = send(hpart.at[other_core], hcore, partner)
    cp.wait_recv()
    hpart[c] = hpart[c] + hcore[...]
    leg = send(hpart.at[c, far], hline.at[0], to_h(near))
    plain = send(hpart.at[c, back], hline.at[1], to_h(back))
    leg.wait_recv()
    hpart[c, near] = hpart[c, near] + hline[0]
    summed = send(hpart.at[c, near], hline.at[2], to_h(near))
    hidden = acc[links[SLOTS + col]] + hcore[h].astype(F32)
    plain.wait_recv()
    hidden = hidden + hline[1].astype(F32)
    summed.wait_recv()
    hidden = hidden + hline[2].astype(F32)

    pre_act = jnp.dot(hidden, weight[...], precision=HIGHEST, preferred_element_type=F32) + bias[...]
    sig = jax.nn.sigmoid(pre_act)
    slope = sig * (1.0 + pre_act * (1.0 - sig))
    grad_pre = (cot[...].astype(F32) * slope).astype(BF16)
    grow[h, c] = grad_pre

    own = grow.at[h, c]
    ahead = send(own, own, to_h(near))
    behind = send(own, own, to_h(back))
    over = [send(own, own, partner)]
    out[...] = (pre_act * sig).astype(BF16)
    factor = 1.0 / math.sqrt(TILE * NY * NZ * NX * NH * NC)
    grad_float = grad_pre.astype(F32)
    local = lax.dot_general(hidden, grad_float, (((0,), (0,)), ((), ())), precision=HIGHEST,
                            preferred_element_type=F32)
    local_bias = jnp.sum(grad_float, axis=0, keepdims=True)
    for cc in range(NC):
        cols = slice(cc * TILE, (cc + 1) * TILE)
        wbuf[cc, :, :, 0:8, :] = local[:, cols].reshape(NX, NY, 8, TILE)
        wbuf[cc, :, :, 8:16, :] = jnp.broadcast_to(local_bias[:, cols].reshape(1, 1, 1, TILE), (NX, NY, 8, TILE))
    ahead.wait_recv()
    block = grow.at[back, c]
    onward = send(block, block, to_h(near))
    over.append(send(block, block, partner))
    behind.wait_recv()
    block = grow.at[near, c]
    over.append(send(block, block, partner))
    w_core = send(wbuf.at[other_core], wcore, partner)
    onward.wait_recv()
    block = grow.at[far, c]
    over.append(send(block, block, partner))
    for cp in over:
        cp.wait_recv()

    for k in range(SLOTS):
        spot = table[0, k]
        value = jnp.dot(flip[k], grow[spot // NC, spot % NC], preferred_element_type=F32)
        acc[k] = value + acc[links[SLOTS + RT + k]]

    def fill(s):
        yd = at_y(s)
        for zi in range(NZ):
            for xi in range(NX):
                place = (yd * NZ + zi) * NX + xi
                part[yd, zi, xi] = acc[links[2 * SLOTS + RT + place]].astype(BF16)

    def add(dst, src):
        dst[...] = dst[...] + src[...]

    def q_start(s):
        way = 1 if s % 2 == 0 else -1
        place = len(lines)
        lines[s] = way, place
        leg = send(part.at[at_y(s), :, at_x(2), SECOND, :], line_q.at[place, 0], to_x(way))
        straight = send(part.at[at_y(s), :, at_x(-way), SECOND, :], line_q.at[place, 1], to_x(-way))
        return leg, straight

    def q_middle(s, leg):
        way, place = lines[s]
        leg.wait_recv()
        block = part.at[at_y(s), :, at_x(way), SECOND, :]
        add(block, line_q.at[place, 0])
        return send(block, line_q.at[place, 2], to_x(way))

    def q_end(s, straight, summed):
        way, place = lines[s]
        straight.wait_recv()
        summed.wait_recv()
        block = part.at[at_y(s), :, x, SECOND, :]
        block[...] = block[...] + line_q[place, 1] + line_q[place, 2]

    lines = {}
    fill(4)
    ring_up = send(part.at[at_y(4), :, 0:2, FIRST, :], ring_p.at[0, 0, :, 0:2], to_y(1))
    ring_down = send(part.at[at_y(4), :, 2:4, FIRST, :], ring_p.at[1, 0, :, 2:4], to_y(-1))
    started = {4: q_start(4)}
    for s in (3, -3, 2, -2, 1, -1, 0):
        fill(s)
        started[s] = q_start(s)
    middle = {4: q_middle(4, started[4][0])}

    w_core.wait_recv()
    add(wbuf.at[c], wcore)
    w_x = [send(wbuf.at[c, at_x(s)], wx.at[s - 1], to_x(s)) for s in (1, 2, 3)]

    q_up = q_down = None
    for t in (0, 1, 2, 3, 4):
        group = [4] if t == 0 else ([4 - t, t - 4] if t < 4 else [0])
        after = [] if t == 4 else ([3 - t, t - 3] if t < 3 else [0])
        for s in after:
            middle[s] = q_middle(s, started[s][0])
        if t >= 1:
            ring_up.wait_recv()
            ring_down.wait_recv()
            if t == 1:
                add(part.at[at_y(3), :, 0:2, FIRST, :], ring_p.at[0, 0, :, 0:2])
                add(part.at[at_y(-3), :, 2:4, FIRST, :], ring_p.at[1, 0, :, 2:4])
            else:
                add(part.at[at_y(4 - t), :, :, FIRST, :], ring_p.at[0, t - 1])
                add(part.at[at_y(t - 4), :, :, FIRST, :], ring_p.at[1, t - 1])
            if t < 4:
                ring_up = send(part.at[at_y(4 - t), :, :, FIRST, :], ring_p.at[0, t], to_y(1))
                ring_down = send(part.at[at_y(t - 4), :, :, FIRST, :], ring_p.at[1, t], to_y(-1))
            else:
                px = [send(part.at[y, :, at_x(s), FIRST, :], line_p.at[s - 1], to_x(s)) for s in (1, 2, 3)]
        for s in group:
            q_end(s, started[s][1], middle[s])
        if t == 0:
            q_up = send(part.at[at_y(4), :, x, pl.ds(CUT, MID - CUT), :],
                        ring_q.at[0, 0, :, pl.ds(0, MID - CUT), :], to_y(1))
            q_down = send(part.at[at_y(4), :, x, pl.ds(MID, TILE - MID), :],
                          ring_q.at[1, 0, :, pl.ds(MID - CUT, TILE - MID), :], to_y(-1))
        else:
            q_up.wait_recv()
            q_down.wait_recv()
            if t == 1:
                add(part.at[at_y(3), :, x, pl.ds(CUT, MID - CUT), :], ring_q.at[0, 0, :, pl.ds(0, MID - CUT), :])
                add(part.at[at_y(-3), :, x, pl.ds(MID, TILE - MID), :],
                    ring_q.at[1, 0, :, pl.ds(MID - CUT, TILE - MID), :])
            else:
                add(part.at[at_y(4 - t), :, x, SECOND, :], ring_q.at[0, t - 1])
                add(part.at[at_y(t - 4), :, x, SECOND, :], ring_q.at[1, t - 1])
            if t < 4:
                q_up = send(part.at[at_y(4 - t), :, x, SECOND, :], ring_q.at[0, t], to_y(1))
                q_down = send(part.at[at_y(t - 4), :, x, SECOND, :], ring_q.at[1, t], to_y(-1))
        if t == 0:
            for cp in w_x:
                cp.wait_recv()
            wbuf[c, x] = wbuf[c, x] + wx[0] + wx[1] + wx[2]
            w_y = [send(wbuf.at[c, x, at_y(s)], wy.at[s - 1], to_y(s)) for s in range(1, NY)]
        elif t == 1:
            for cp in w_y:
                cp.wait_recv()
            wz[z] = wbuf[c, x, y] + jnp.sum(wy[...], axis=0)
            w_z = [send(wz.at[z], wz.at[z], to_z(s)) for s in (1, 2)]
        elif t == 2:
            for cp in w_z:
                cp.wait_recv()
            wh[h] = wz[0] + wz[1] + wz[2]
            w_h = [send(wh.at[h], wh.at[h], to_h(at_h(s))) for s in (1, 2, 3)]
        elif t == 3:
            for cp in w_h:
                cp.wait_recv()
            wout[c, x, y] = (wh[0] + wh[1] + wh[2] + wh[3]) * factor
            piece = wout.at[c, x, y]
            w_y = [send(piece, piece, to_y(s)) for s in range(1, NY)]
        else:
            for cp in w_y:
                cp.wait_recv()
            piece = wout.at[c, x]
            w_x = [send(piece, piece, to_x(s)) for s in (1, 2, 3)]
    for cp in px:
        cp.wait_recv()
    block = part.at[y, :, x, FIRST, :]
    block[...] = block[...] + line_p[0] + line_p[1] + line_p[2]
    last = [send(part.at[y, at_z(s), x], zline.at[s - 1], to_z(s)) for s in (1, 2)]
    for cp in w_x:
        cp.wait_recv()
    w_core = send(wout.at[c], wout.at[c], partner)
    for cp in last:
        cp.wait_recv()
    adjoint = part[y, z, x].astype(F32) + zline[0].astype(F32) + zline[1].astype(F32)
    gin[...] = lax.dot_general(adjoint, weight[...], (((1,), (1,)), ((), ())), precision=HIGHEST,
                               preferred_element_type=F32).astype(BF16)
    w_core.wait_recv()
    for cc in range(NC):
        cols = slice(cc * TILE, (cc + 1) * TILE)
        gw[:, cols] = wout[cc, :, :, 0:8, :].reshape(FEAT, TILE)
        gb[:, cols] = wout[cc, 0, 0, 8:9, :]
    for cp in copies:
        cp.wait_send()


def per_device(features, weight, bias, cotangent, tile_values, tile_pos, tile_count):
    places = tile_pos[0, 0]
    in_use = tile_count[0, 0]
    slot = jnp.arange(SLOTS, dtype=jnp.int32)
    rows, cols = places // CT, places % CT
    full = jnp.full((CT,), SLOTS, jnp.int32)
    asked = jnp.concatenate([rows, jnp.arange(RT, dtype=jnp.int32), cols + RT, jnp.arange(CT, dtype=jnp.int32) + RT])
    limit = jnp.concatenate([slot, full[:RT], slot, full])
    limit = jnp.minimum(limit, in_use)
    same = jnp.where(asked[:, None] < RT, rows[None, :] == asked[:, None], cols[None, :] + RT == asked[:, None])
    found = jnp.max(jnp.where(same & (slot[None, :] < limit[:, None]), slot[None, :], -1), axis=1)
    links = jnp.where(found < 0, SLOTS, found)
    table = jnp.stack([rows, cols])
    vmem = pl.BlockSpec(memory_space=pltpu.VMEM)
    smem = pl.BlockSpec(memory_space=pltpu.SMEM)
    blocks = pltpu.VMEM
    scratch = [
        blocks((NY, NZ, NX, TILE, FEAT), BF16),
        blocks((SLOTS, TILE, TILE), BF16),
        blocks((SLOTS + 1, TILE, FEAT), F32),
        blocks((NY, NZ, NX, TILE, FEAT), BF16),
        blocks((NC, NH, TILE, FEAT), BF16),
        blocks((NH, TILE, FEAT), BF16),
        blocks((3, TILE, FEAT), BF16),
        blocks((NH, NC, TILE, FEAT), BF16),
        blocks((2, 4, NZ, NX, CUT, FEAT), BF16),
        blocks((3, NZ, CUT, FEAT), BF16),
        blocks((NY, 3, NZ, TILE - CUT, FEAT), BF16),
        blocks((2, 4, NZ, TILE - CUT, FEAT), BF16),
        blocks((2, TILE, FEAT), BF16),
        blocks((NC, NX, NY, 16, TILE), F32),
        blocks((NX, NY, 16, TILE), F32),
        blocks((3, NY, 16, TILE), F32),
        blocks((NY - 1, 16, TILE), F32),
        blocks((NZ, 16, TILE), F32),
        blocks((NH, 16, TILE), F32),
        blocks((NC, NX, NY, 16, TILE), F32),
        pltpu.SemaphoreType.DMA((NSEM,)),
        pltpu.SemaphoreType.DMA((NSEM,)),
    ]
    output, grad_weight, grad_bias, grad_input = pl.pallas_call(
        kernel,
        out_shape=(
            jax.ShapeDtypeStruct((TILE, FEAT), BF16),
            jax.ShapeDtypeStruct((FEAT, FEAT), F32),
            jax.ShapeDtypeStruct((1, FEAT), F32),
            jax.ShapeDtypeStruct((TILE, FEAT), BF16),
        ),
        in_specs=[smem, smem] + [vmem] * 5,
        out_specs=(vmem,) * 4,
        scratch_shapes=scratch,
        compiler_params=pltpu.CompilerParams(
            collective_id=0, has_side_effects=True, vmem_limit_bytes=48 * 1024 * 1024),
    )(table, links, features, weight, bias.reshape(1, FEAT), cotangent, tile_values[0, 0])
    return output, grad_weight, grad_bias[0], grad_input


def solution(mesh):
    in_specs = (
        P(("row", "col"), None),
        P(),
        P(),
        P(("row", "col"), None),
        P("row", "col", None, None, None),
        P("row", "col", None),
        P("row", "col"),
    )
    out_specs = (P(("row", "col"), None), P(), P(), P(("row", "col"), None))
    return jax.shard_map(
        per_device, mesh=mesh, in_specs=in_specs, out_specs=out_specs, check_vma=False
    )
```

time: 1740 us -> 172 us (0.10)
  waiting for transfers between devices: 1550 us -> 0 us
  Pallas kernels: 0 us -> 162 us
  blocking collectives: 130 us -> 0 us
    psum x1 -> x0, waiting for transfers between devices: 590 us -> none  [per_device(): lax.psum((local_weight, local_bias), ('row', 'col'))]
    reduce_scatter x2 -> x0, waiting for transfers between devices: 517 us -> none  [the longest x1 356 us: per_device(): adjoint = lax.psum_scatter(backward, 'row', scatter_dimension=0, tiled=True)]
    all_gather x1 -> x0, waiting for transfers between devices: 442 us -> none  [per_device(): lax.all_gather(features, 'row', axis=0, tiled=True)]
    pallas_call x0 -> x1, Pallas kernels: none -> 162 us  [per_device(): pl.pallas_call(kernel, out_shape=(jax.ShapeDtypeStruct((TILE, FEAT), BF16...]
    psum x1 -> x0, blocking collectives: 109 us -> none  [per_device(): lax.psum((local_weight, local_bias), ('row', 'col'))]
    all_gather x1 -> x0, blocking collectives: 20.8 us -> none  [per_device(): block_dpre = lax.all_gather(grad_pre, 'col', axis=0, tiled=True)]
  transfers between devices with their start and end apart: 4 -> 0, of which waited for: 4 -> 0; matrix products, arithmetic and copies ran while one was open for 0% -> 0% of each run, Pallas kernels for 0% -> 0%
where the time goes in v1:
time: 172 us
  Pallas kernels  162 us (94%)
  local copies, waits for them, and re-layouts  7.61 us (4%)
    pallas_call x1, Pallas kernels, per_device(): pl.pallas_call(kernel, out_shape=(jax.ShapeDtypeStruct((TILE, FEAT), BF16...  162 us
    unnamed x16, local copies, waits for them, and re-layouts  7.6 us

profile of v1, /device:TPU:1, one launch (start us, length us, event | category | flops | bytes accessed | tf_op | source)
XLA Modules:
  0.0 171.5 jit_solution(10838386468774564080)
XLA Ops:
  1.3 0.1 add_minimum_fusion
  1.4 0.0 copy-start.5
  1.4 0.7 copy-done.5
  2.1 0.1 broadcast_compare_fusion
  2.2 0.1 select_reduce_fusion
  2.3 0.0 copy-start.4
  2.3 0.7 copy-done.4
  3.0 0.0 copy-start
  3.0 1.1 copy-done
  4.1 0.0 copy-start.1
  4.1 0.9 copy-done.1
  5.0 0.0 copy-start.2
  5.1 0.8 copy-done.2
  5.9 0.0 copy-start.3
  5.9 0.8 copy-done.3
  6.7 162.2 %shard_map.102 = (bf16[128,256]{1,0:T(8,128)(2,1)S(1)}, f32[256,256]{1,0:T(8,128)S(1)}, f32[1,256]{1,0:T(1,128)S(1)}, bf16[128,256]{1,0:T(8,128)(2,1)S(1)}) custom-call(s32[2,24]{1,0:T(2,128)S(1)} %pad_add_fusion.table, s32[152]{0:T(256)S(1)} %compare_select_fusion.links, bf16[128,256]{1,0:T(8,128)(2,1)S(1)} %copy-done.2, f32[256,256]{1,0:T(8,128)S(1)} %copy-done.1, ...), custom_call_target="tpu_custom_call" | custom-call | tf_op jit(solution)/shard_map/pallas_call | solution.py:388
  169.0 0.6 copy.16
  169.6 0.7 copy.17
  170.3 0.6 copy.18
  170.9 0.6 copy.19
  (9 shorter events, 0.1 us)
Async XLA Ops:
  1.4 0.7 copy-start.5
  2.3 0.7 copy-start.4
  3.0 1.1 copy-start
  4.1 0.9 copy-start.1
  5.0 0.8 copy-start.2
  5.9 0.8 copy-start.3

commit v2 on v1

v2 whole, which is shorter than its diff:
```python
import math

import jax
import jax.numpy as jnp
from jax import lax
from jax.experimental import pallas as pl
from jax.experimental.pallas import tpu as pltpu
from jax.sharding import PartitionSpec as P

TILE = 128
FEAT = 256
NY, NZ, NX = 8, 3, 4
NH, NC = 4, 2
SLOTS = 24
RT = NH * NC
CT = NY * NZ * NX
NSEM = 240
MESH = pl.DeviceIdType.MESH
HIGHEST = lax.Precision.HIGHEST
F32 = jnp.float32
BF16 = jnp.bfloat16
FIRST = pl.ds(0, 32)
SECOND = pl.ds(32, 64)
UPPER = pl.ds(32, 32)
LOWER = pl.ds(64, 32)
THIRD = pl.ds(96, 32)
AHEAD = pl.ds(0, 96)
GROUPS = ((4,), (3, -3), (2, -2), (1, -1), (0,))


def way_of(s):
    return 1 if s > 0 else -1


def kernel(places, links, feat_in, weight_in, bias_in, cot_in, vals_in, out_to, gw_to, gb_to, gin_to,
           out, gw, gb, gin, weight, bias, cot, vals,
           gath, flip, acc, part, hpart, hcore, hline, grow,
           ring_p, line_p, line_q, ring_q, line_c, ring_c, last_c, zline,
           wbuf, wcore, wx, wy, wz, wh, wout, ssem, rsem, lsem):
    row = lax.axis_index("row")
    col = lax.axis_index("col")
    y, z, x = row // (NZ * NX), (row // NX) % NZ, row % NX
    h, c = col // NC, col % NC

    def at_x(s):
        return lax.rem(x + s + NX, NX)

    def at_y(s):
        return lax.rem(y + s + NY, NY)

    def at_z(s):
        return lax.rem(z + s, NZ)

    def at_h(s):
        return lax.rem(h + s + NH, NH)

    def to_x(s):
        return ((y * NZ + z) * NX + at_x(s), col)

    def to_y(s):
        return ((at_y(s) * NZ + z) * NX + x, col)

    def to_z(s):
        return ((y * NZ + at_z(s)) * NX + x, col)

    def to_h(index):
        return (row, index * NC + c)

    other_core = 1 - c
    partner = (row, h * NC + other_core)
    turn = 1 - 2 * c
    near = at_h(turn)
    back = at_h(-turn)
    far = at_h(2)

    copies = []

    def send(src, dst, target):
        index = len(copies)
        copy = pltpu.make_async_remote_copy(
            src_ref=src, dst_ref=dst, send_sem=ssem.at[index], recv_sem=rsem.at[index],
            device_id=target, device_id_type=MESH)
        copy.start()
        copies.append(copy)
        return copy

    def fetch(src, dst, index):
        copy = pltpu.make_async_copy(src, dst, lsem.at[index])
        copy.start()
        return copy

    barrier = pltpu.get_barrier_semaphore()
    friends = [to_x(s) for s in (1, 2, 3)] + [to_y(s) for s in range(1, NY)]
    friends += [to_z(s) for s in (1, 2)] + [to_h(at_h(s)) for s in (1, 2, 3)] + [partner]
    for friend in friends:
        pl.semaphore_signal(barrier, inc=1, device_id=friend, device_id_type=MESH)
    own_copy = fetch(feat_in, gath.at[y, z, x], 0)
    fetched = [fetch(vals_in, vals, 1), fetch(weight_in, weight, 2), fetch(cot_in, cot, 3), fetch(bias_in, bias, 4)]
    acc[SLOTS] = jnp.zeros((TILE, FEAT), F32)
    own_copy.wait()
    pl.semaphore_wait(barrier, len(friends))

    def both(up, down):
        return send(up, up, to_y(1)), send(down, down, to_y(-1))

    def ring(view, half, s, arrived):
        for cp in arrived:
            cp.wait_recv()
        if s < 3:
            return both(view(at_y(-s)), view(at_y(s)))
        if s == 3:
            return both(half(at_y(-s), 0), half(at_y(s), 1))
        return None

    def p_view(yd):
        return gath.at[yd, :, :, FIRST, :]

    def p_half(yd, i):
        return gath.at[yd, :, 2 * i:2 * i + 2, FIRST, :]

    def q_view(yd):
        return gath.at[yd, :, x, SECOND, :]

    def q_half(yd, i):
        return gath.at[yd, :, x, (UPPER, LOWER)[i], :]

    def c_view(yd):
        return gath.at[yd, z, :, THIRD, :]

    def c_half(yd, i):
        return gath.at[yd, z, 2 * i:2 * i + 2, THIRD, :]

    def q_direct(s):
        block = gath.at[at_y(s), :, x, SECOND, :]
        return {1: send(block, block, to_x(1)), -1: send(block, block, to_x(-1))}

    def q_forward(s, arrived):
        way = way_of(s)
        arrived[way].wait_recv()
        block = gath.at[at_y(s), :, at_x(-way), SECOND, :]
        return [arrived[-way], send(block, block, to_x(way))]

    def c_direct(s):
        block = gath.at[at_y(s), z, :, THIRD, :]
        return [send(block, block, to_z(1)), send(block, block, to_z(2))]

    own = gath.at[y, z, x, AHEAD, :]
    zs = [send(own, own, to_z(s)) for s in (1, 2)]
    own = gath.at[y, z, x, THIRD, :]
    xs = [send(own, own, to_x(s)) for s in (1, 2, 3)]
    pending = []
    for cp in zs:
        cp.wait_recv()
    q_ring = both(q_view(y), q_view(y))
    own = gath.at[y, :, x, FIRST, :]
    px = [send(own, own, to_x(s)) for s in (1, 2, 3)]
    for cp in xs:
        cp.wait_recv()
    c_ring = both(c_view(y), c_view(y))
    direct = {0: q_direct(0)}
    pending += c_direct(0)
    fetched[0].wait()
    p_ring = None
    for s in (1, 2, 3, 4):
        current = GROUPS[4 - s]
        q_ring = ring(q_view, q_half, s, q_ring)
        for t in current:
            direct[t] = q_direct(t)
        c_ring = ring(c_view, c_half, s, c_ring)
        for t in current:
            pending += c_direct(t)
        if s == 1:
            for cp in px:
                cp.wait_recv()
            p_ring = both(p_view(y), p_view(y))
        for t in GROUPS[5 - s]:
            pending += q_forward(t, direct[t])
        if s > 1:
            p_ring = ring(p_view, p_half, s - 1, p_ring)
        for k in range(6 * s - 6, 6 * s):
            flip[k] = vals[k].T
    pending += q_forward(4, direct[4])
    ring(p_view, p_half, 4, p_ring)
    for cp in pending:
        cp.wait_recv()

    for k in range(SLOTS):
        spot = places[k] % CT
        block = gath[spot // (NZ * NX), (spot // NX) % NZ, spot % NX]
        value = jnp.dot(vals[k], block, preferred_element_type=F32)
        acc[k] = value + acc[links[k]]
    for r in range(RT):
        hpart[r % NC, r // NC] = acc[links[SLOTS + r]].astype(BF16)

    cp = send(hpart.at[other_core], hcore, partner)
    cp.wait_recv()
    hpart[c] = hpart[c] + hcore[...]
    leg = send(hpart.at[c, far], hline.at[0], to_h(near))
    plain = send(hpart.at[c, back], hline.at[1], to_h(back))
    leg.wait_recv()
    hpart[c, near] = hpart[c, near] + hline[0]
    summed = send(hpart.at[c, near], hline.at[2], to_h(near))
    hidden = acc[links[SLOTS + col]] + hcore[h].astype(F32)
    plain.wait_recv()
    hidden = hidden + hline[1].astype(F32)
    summed.wait_recv()
    hidden = hidden + hline[2].astype(F32)

    for cp in fetched[1:]:
        cp.wait()
    pre_act = jnp.dot(hidden, weight[...], precision=HIGHEST, preferred_element_type=F32) + bias[...]
    sig = jax.nn.sigmoid(pre_act)
    slope = sig * (1.0 + pre_act * (1.0 - sig))
    grad_pre = (cot[...].astype(F32) * slope).astype(BF16)
    grow[h, c] = grad_pre

    own = grow.at[h, c]
    ahead = send(own, own, to_h(near))
    behind = send(own, own, to_h(back))
    over = [send(own, own, partner)]
    out[...] = (pre_act * sig).astype(BF16)
    stored = [fetch(out, out_to, 5)]
    factor = 1.0 / math.sqrt(TILE * NY * NZ * NX * NH * NC)
    grad_float = grad_pre.astype(F32)
    local = lax.dot_general(hidden, grad_float, (((0,), (0,)), ((), ())), precision=HIGHEST,
                            preferred_element_type=F32)
    local_bias = jnp.sum(grad_float, axis=0, keepdims=True)
    for cc in range(NC):
        cols = slice(cc * TILE, (cc + 1) * TILE)
        wbuf[cc, :, :, 0:8, :] = local[:, cols].reshape(NX, NY, 8, TILE)
        wbuf[cc, :, :, 8:16, :] = jnp.broadcast_to(local_bias[:, cols].reshape(1, 1, 1, TILE), (NX, NY, 8, TILE))
    w_core = send(wbuf.at[other_core], wcore, partner)
    ahead.wait_recv()
    block = grow.at[back, c]
    onward = send(block, block, to_h(near))
    over.append(send(block, block, partner))
    behind.wait_recv()
    block = grow.at[near, c]
    over.append(send(block, block, partner))
    w_core.wait_recv()
    wbuf[c] = wbuf[c] + wcore[...]
    w_x = [send(wbuf.at[c, at_x(s)], wx.at[s - 1], to_x(s)) for s in (1, 2, 3)]
    onward.wait_recv()
    block = grow.at[far, c]
    over.append(send(block, block, partner))
    for cp in w_x:
        cp.wait_recv()
    wbuf[c, x] = wbuf[c, x] + wx[0] + wx[1] + wx[2]
    w_y = [send(wbuf.at[c, x, at_y(s)], wy.at[s - 1], to_y(s)) for s in range(1, NY)]
    for cp in over:
        cp.wait_recv()

    for k in range(SLOTS):
        spot = places[k] // CT
        value = jnp.dot(flip[k], grow[spot // NC, spot % NC], preferred_element_type=F32)
        acc[k] = value + acc[links[SLOTS + RT + k]]

    def fill(s):
        yd = at_y(s)
        for zi in range(NZ):
            for xi in range(NX):
                place = (yd * NZ + zi) * NX + xi
                part[yd, zi, xi] = acc[links[2 * SLOTS + RT + place]].astype(BF16)

    def add(dst, src):
        dst[...] = dst[...] + src[...]

    def add3(dst, one, two):
        dst[...] = (dst[...].astype(F32) + one[...].astype(F32) + two[...].astype(F32)).astype(BF16)

    def q_start(s):
        way, place = way_of(s), len(started)
        leg = send(part.at[at_y(s), :, at_x(2), SECOND, :], line_q.at[place, 0], to_x(way))
        straight = send(part.at[at_y(s), :, at_x(-way), SECOND, :], line_q.at[place, 1], to_x(-way))
        lines = [send(part.at[at_y(s), at_z(d), :, THIRD, :], line_c.at[place, d - 1], to_z(d)) for d in (1, 2)]
        started[s] = place, leg, straight, lines

    def q_middle(s):
        way = way_of(s)
        place, leg, _, _ = started[s]
        leg.wait_recv()
        block = part.at[at_y(s), :, at_x(way), SECOND, :]
        add(block, line_q.at[place, 0])
        middle[s] = send(block, line_q.at[place, 2], to_x(way))

    def q_end(s):
        place, _, straight, _ = started[s]
        straight.wait_recv()
        middle[s].wait_recv()
        add3(part.at[at_y(s), :, x, SECOND, :], line_q.at[place, 1], line_q.at[place, 2])

    def c_end(s):
        place, _, _, lines = started[s]
        for cp in lines:
            cp.wait_recv()
        add3(part.at[at_y(s), z, :, THIRD, :], line_c.at[place, 0], line_c.at[place, 1])

    def ring_sum(view, half, slot, slot_half, t, arrived):
        if t >= 1:
            for cp in arrived:
                cp.wait_recv()
            if t == 1:
                add(half(at_y(3), 0), slot_half(0))
                add(half(at_y(-3), 1), slot_half(1))
            elif t < 4:
                add(view(at_y(4 - t)), slot(0, t - 1))
                add(view(at_y(t - 4)), slot(1, t - 1))
            else:
                add3(view(y), slot(0, 3), slot(1, 3))
        if t == 0:
            return send(half(at_y(4), 0), slot_half(0), to_y(1)), send(half(at_y(4), 1), slot_half(1), to_y(-1))
        if t < 4:
            return (send(view(at_y(4 - t)), slot(0, t), to_y(1)), send(view(at_y(t - 4)), slot(1, t), to_y(-1)))
        return None

    p_args = (lambda yd: part.at[yd, :, :, FIRST, :],
              lambda yd, i: part.at[yd, :, 2 * i:2 * i + 2, FIRST, :],
              lambda i, t: ring_p.at[i, t],
              lambda i: ring_p.at[i, 0, :, 2 * i:2 * i + 2])
    q_args = (lambda yd: part.at[yd, :, x, SECOND, :],
              lambda yd, i: part.at[yd, :, x, (UPPER, LOWER)[i], :],
              lambda i, t: ring_q.at[i, t],
              lambda i: ring_q.at[i, 0, :, pl.ds(32 * i, 32)])
    c_args = (lambda yd: part.at[yd, z, :, THIRD, :],
              lambda yd, i: part.at[yd, z, 2 * i:2 * i + 2, THIRD, :],
              lambda i, t: ring_c.at[i, t],
              lambda i: ring_c.at[i, 0, 2 * i:2 * i + 2])
    started, middle = {}, {}
    fill(4)
    p_ring = ring_sum(*p_args, 0, None)
    q_start(4)
    for group in GROUPS[1:]:
        for s in group:
            fill(s)
        if group[0] == 3:
            for s in group:
                q_start(s)
    q_middle(4)

    for cp in w_y:
        cp.wait_recv()
    wz[z] = wbuf[c, x, y] + jnp.sum(wy[...], axis=0)
    w_z = [send(wz.at[z], wz.at[z], to_z(s)) for s in (1, 2)]

    q_ring = c_ring = None
    for t in (0, 1, 2, 3, 4):
        if t < 3:
            for s in GROUPS[t + 2]:
                q_start(s)
        if t >= 1:
            p_ring = ring_sum(*p_args, t, p_ring)
        if t == 4:
            px = [send(part.at[y, :, at_x(s), FIRST, :], line_p.at[s - 1], to_x(s)) for s in (1, 2, 3)]
        for s in GROUPS[t]:
            c_end(s)
        c_ring = ring_sum(*c_args, t, c_ring)
        for s in GROUPS[t]:
            q_end(s)
        q_ring = ring_sum(*q_args, t, q_ring)
        if t < 4:
            for s in GROUPS[t + 1]:
                q_middle(s)
        if t == 0:
            for cp in w_z:
                cp.wait_recv()
            wh[h] = wz[0] + wz[1] + wz[2]
            w_h = [send(wh.at[h], wh.at[h], to_h(at_h(s))) for s in (1, 2, 3)]
        elif t == 1:
            for cp in w_h:
                cp.wait_recv()
            wout[c, x, y] = (wh[0] + wh[1] + wh[2] + wh[3]) * factor
            piece = wout.at[c, x, y]
            w_y = [send(piece, piece, to_y(s)) for s in range(1, NY)]
        elif t == 2:
            for cp in w_y:
                cp.wait_recv()
            piece = wout.at[c, x]
            w_x = [send(piece, piece, to_x(s)) for s in (1, 2, 3)]
        elif t == 3:
            for cp in w_x:
                cp.wait_recv()
            w_core = send(wout.at[c], wout.at[c], partner)
    last_q = [send(part.at[y, at_z(s), x, SECOND, :], zline.at[s - 1, SECOND, :], to_z(s)) for s in (1, 2)]
    last_x = [send(part.at[y, z, at_x(s), THIRD, :], last_c.at[s - 1], to_x(s)) for s in (1, 2, 3)]
    for cp in px:
        cp.wait_recv()
    block = part.at[y, :, x, FIRST, :]
    block[...] = (block[...].astype(F32) + line_p[0].astype(F32) + line_p[1].astype(F32)
                  + line_p[2].astype(F32)).astype(BF16)
    last_p = [send(part.at[y, at_z(s), x, FIRST, :], zline.at[s - 1, FIRST, :], to_z(s)) for s in (1, 2)]
    w_core.wait_recv()
    for cc in range(NC):
        cols = slice(cc * TILE, (cc + 1) * TILE)
        gw[:, cols] = wout[cc, :, :, 0:8, :].reshape(FEAT, TILE)
        gb[:, cols] = wout[cc, 0, 0, 8:9, :]
    stored += [fetch(gw, gw_to, 7), fetch(gb, gb_to, 8)]
    for cp in last_q + last_x + last_p:
        cp.wait_recv()
    ahead_rows = part[y, z, x, AHEAD, :].astype(F32) + zline[0].astype(F32) + zline[1].astype(F32)
    third_rows = part[y, z, x, THIRD, :].astype(F32) + last_c[0].astype(F32) + last_c[1].astype(F32)
    third_rows = third_rows + last_c[2].astype(F32)
    adjoint = jnp.concatenate([ahead_rows, third_rows], axis=0)
    gin[...] = lax.dot_general(adjoint, weight[...], (((1,), (1,)), ((), ())), precision=HIGHEST,
                               preferred_element_type=F32).astype(BF16)
    stored.append(fetch(gin, gin_to, 6))
    for cp in copies:
        cp.wait_send()
    for cp in stored:
        cp.wait()


def hand_over(*refs):
    given, wanted, kept, sems = refs[0:4], refs[4:8], refs[8:12], refs[12]
    moves = [pltpu.make_async_copy(given[i], kept[i], sems.at[i]) for i in range(4)]
    for move in moves:
        move.start()
    for i in range(4):
        moves[i].wait()
        moves.append(pltpu.make_async_copy(kept[i], wanted[i], sems.at[4 + i]))
        moves[4 + i].start()
    for move in moves[4:]:
        move.wait()


def per_device(features, weight, bias, cotangent, tile_values, tile_pos, tile_count):
    places = tile_pos[0, 0]
    in_use = tile_count[0, 0]
    slot = jnp.arange(SLOTS, dtype=jnp.int32)
    rows, cols = places // CT, places % CT
    full = jnp.full((CT,), SLOTS, jnp.int32)
    asked = jnp.concatenate([rows, jnp.arange(RT, dtype=jnp.int32), cols + RT, jnp.arange(CT, dtype=jnp.int32) + RT])
    limit = jnp.concatenate([slot, full[:RT], slot, full])
    limit = jnp.minimum(limit, in_use)
    same = jnp.where(asked[:, None] < RT, rows[None, :] == asked[:, None], cols[None, :] + RT == asked[:, None])
    found = jnp.max(jnp.where(same & (slot[None, :] < limit[:, None]), slot[None, :], -1), axis=1)
    links = jnp.where(found < 0, SLOTS, found)
    smem = pl.BlockSpec(memory_space=pltpu.SMEM)
    blocks = pltpu.VMEM
    scratch = [
        blocks((TILE, FEAT), BF16),
        blocks((FEAT, FEAT), F32),
        blocks((1, FEAT), F32),
        blocks((TILE, FEAT), BF16),
        blocks((FEAT, FEAT), F32),
        blocks((1, FEAT), F32),
        blocks((TILE, FEAT), BF16),
        blocks((SLOTS, TILE, TILE), BF16),
        blocks((NY, NZ, NX, TILE, FEAT), BF16),
        blocks((SLOTS, TILE, TILE), BF16),
        blocks((SLOTS + 1, TILE, FEAT), F32),
        blocks((NY, NZ, NX, TILE, FEAT), BF16),
        blocks((NC, NH, TILE, FEAT), BF16),
        blocks((NH, TILE, FEAT), BF16),
        blocks((3, TILE, FEAT), BF16),
        blocks((NH, NC, TILE, FEAT), BF16),
        blocks((2, 4, NZ, NX, 32, FEAT), BF16),
        blocks((3, NZ, 32, FEAT), BF16),
        blocks((NY, 3, NZ, 64, FEAT), BF16),
        blocks((2, 4, NZ, 64, FEAT), BF16),
        blocks((NY, 2, NX, 32, FEAT), BF16),
        blocks((2, 4, NX, 32, FEAT), BF16),
        blocks((3, 32, FEAT), BF16),
        blocks((2, 96, FEAT), BF16),
        blocks((NC, NX, NY, 16, TILE), F32),
        blocks((NX, NY, 16, TILE), F32),
        blocks((3, NY, 16, TILE), F32),
        blocks((NY - 1, 16, TILE), F32),
        blocks((NZ, 16, TILE), F32),
        blocks((NH, 16, TILE), F32),
        blocks((NC, NX, NY, 16, TILE), F32),
        pltpu.SemaphoreType.DMA((NSEM,)),
        pltpu.SemaphoreType.DMA((NSEM,)),
        pltpu.SemaphoreType.DMA((9,)),
    ]
    results = (
        jax.ShapeDtypeStruct((TILE, FEAT), BF16),
        jax.ShapeDtypeStruct((FEAT, FEAT), F32),
        jax.ShapeDtypeStruct((1, FEAT), F32),
        jax.ShapeDtypeStruct((TILE, FEAT), BF16),
    )
    anywhere = pl.BlockSpec(memory_space=pl.ANY)
    made = pl.pallas_call(
        kernel,
        out_shape=results,
        in_specs=[smem, smem] + [anywhere] * 5,
        out_specs=(anywhere,) * 4,
        scratch_shapes=scratch,
        compiler_params=pltpu.CompilerParams(
            collective_id=0, has_side_effects=True, vmem_limit_bytes=63 * 1024 * 1024),
    )(places, links, features, weight, bias.reshape(1, FEAT), cotangent, tile_values[0, 0])
    output, grad_weight, grad_bias, grad_input = pl.pallas_call(
        hand_over,
        out_shape=results,
        in_specs=[anywhere] * 4,
        out_specs=(anywhere,) * 4,
        scratch_shapes=scratch[:4] + [pltpu.SemaphoreType.DMA((8,))],
    )(*made)
    return output, grad_weight, grad_bias[0], grad_input


def solution(mesh):
    in_specs = (
        P(("row", "col"), None),
        P(),
        P(),
        P(("row", "col"), None),
        P("row", "col", None, None, None),
        P("row", "col", None),
        P("row", "col"),
    )
    out_specs = (P(("row", "col"), None), P(), P(), P(("row", "col"), None))
    return jax.shard_map(
        per_device, mesh=mesh, in_specs=in_specs, out_specs=out_specs, check_vma=False
    )
```

time: 172 us -> 135 us (0.78)
  Pallas kernels: 162 us -> 132 us
  local copies, waits for them, and re-layouts: 7.61 us -> 0.66 us
    pallas_call x1 -> x2, Pallas kernels: 162 us -> 132 us  [the longest x1 130 us: per_device(): pl.pallas_call(kernel, out_shape=results, in_specs=[smem, smem] + [anywhe...]
    unnamed x16 -> x2, local copies, waits for them, and re-layouts: 7.6 us -> 0.65 us
where the time goes in v2:
time: 135 us
  Pallas kernels  132 us (98%)
    pallas_call x1, Pallas kernels, per_device(): pl.pallas_call(kernel, out_shape=results, in_specs=[smem, smem] + [anywhe...  130 us

profile of v2, /device:TPU:1, one launch (start us, length us, event | category | flops | bytes accessed | tf_op | source)
XLA Modules:
  0.0 135.0 jit_solution(4917552780702621638)
XLA Ops:
  1.3 0.1 add_minimum_fusion
  1.4 0.0 copy-start
  1.4 0.7 copy-done
  2.1 0.1 broadcast_compare_fusion
  2.2 0.1 select_reduce_fusion
  2.2 0.6 compare_select_fusion.links
  2.8 130.4 %shard_map.102 = (bf16[128,256]{1,0:T(8,128)(2,1)}, f32[256,256]{1,0:T(8,128)}, f32[1,256]{1,0:T(1,128)}, bf16[128,256]{1,0:T(8,128)(2,1)}) custom-call(s32[24]{0:T(128)} %bitcast.10, s32[152]{0:T(256)} %compare_select_fusion.links, bf16[128,256]{1,0:T(8,128)(2,1)} %feat_in.1, f32[256,256]{1,0:T(8,128)} %weight_in.1, f32[1,256]{1,0:T(1,128)} %bitcast.9, ...), custom_call_target="tpu_custom_call" | custom-call | tf_op jit(solution)/shard_map/pallas_call | solution.py:482
  133.2 1.8 %shard_map.103 = (bf16[128,256]{1,0:T(8,128)(2,1)}, f32[256,256]{1,0:T(8,128)}, f32[1,256]{1,0:T(1,128)}, bf16[128,256]{1,0:T(8,128)(2,1)}) custom-call(bf16[128,256]{1,0:T(8,128)(2,1)} %get-tuple-element.12.refs_0_, f32[256,256]{1,0:T(8,128)} %get-tuple-element.13.refs_1_, f32[1,256]{1,0:T(1,128)} %get-tuple-element.14.refs_2_, ...), custom_call_target="tpu_custom_call" | custom-call | tf_op jit(solution)/shard_map/pallas_call | solution.py:491
  (6 shorter events, 0.0 us)
Async XLA Ops:
  1.4 0.7 copy-start

commit v3 on v2

--- a/solution.py
+++ b/solution.py
@@ -25,6 +25,7 @@
 LOWER = pl.ds(64, 32)
 THIRD = pl.ds(96, 32)
 AHEAD = pl.ds(0, 96)
+HALVES = (pl.ds(0, 64), pl.ds(64, 64))
 GROUPS = ((4,), (3, -3), (2, -2), (1, -1), (0,))
 
 
@@ -32,9 +33,20 @@
     return 1 if s > 0 else -1
 
 
+def split(values):
+    high = values.astype(BF16)
+    return high, (values - high.astype(F32)).astype(BF16)
+
+
+def split_dot(values, high, low):
+    top, rest = split(values)
+    small = jnp.dot(top, low, preferred_element_type=F32) + jnp.dot(rest, high, preferred_element_type=F32)
+    return jnp.dot(top, high, preferred_element_type=F32) + small
+
+
 def kernel(places, links, feat_in, weight_in, bias_in, cot_in, vals_in, out_to, gw_to, gb_to, gin_to,
            out, gw, gb, gin, weight, bias, cot, vals,
-           gath, flip, acc, part, hpart, hcore, hline, grow,
+           wsplit, gath, flip, acc, part, hpart, hcore, hline, grow,
            ring_p, line_p, line_q, ring_q, line_c, ring_c, last_c, zline,
            wbuf, wcore, wx, wy, wz, wh, wout, ssem, rsem, lsem):
     row = lax.axis_index("row")
@@ -159,7 +171,11 @@
     c_ring = both(c_view(y), c_view(y))
     direct = {0: q_direct(0)}
     pending += c_direct(0)
-    fetched[0].wait()
+    for cp in fetched:
+        cp.wait()
+    turned = weight[...].T
+    wsplit[0], wsplit[1] = split(weight[...])
+    wsplit[2], wsplit[3] = split(turned)
     p_ring = None
     for s in (1, 2, 3, 4):
         current = GROUPS[4 - s]
@@ -177,8 +193,6 @@
             pending += q_forward(t, direct[t])
         if s > 1:
             p_ring = ring(p_view, p_half, s - 1, p_ring)
-        for k in range(6 * s - 6, 6 * s):
-            flip[k] = vals[k].T
     pending += q_forward(4, direct[4])
     ring(p_view, p_half, 4, p_ring)
     for cp in pending:
@@ -193,33 +207,43 @@
         hpart[r % NC, r // NC] = acc[links[SLOTS + r]].astype(BF16)
 
     cp = send(hpart.at[other_core], hcore, partner)
+    for k in range(0, 8):
+        flip[k] = vals[k].T
     cp.wait_recv()
     hpart[c] = hpart[c] + hcore[...]
-    leg = send(hpart.at[c, far], hline.at[0], to_h(near))
+    legs = [send(hpart.at[c, far, half, :], hline.at[0, half, :], to_h(near)) for half in HALVES]
+    for k in range(8, 16):
+        flip[k] = vals[k].T
     plain = send(hpart.at[c, back], hline.at[1], to_h(back))
-    leg.wait_recv()
-    hpart[c, near] = hpart[c, near] + hline[0]
-    summed = send(hpart.at[c, near], hline.at[2], to_h(near))
+    summed = []
+    for leg, half in zip(legs, HALVES):
+        leg.wait_recv()
+        hpart[c, near, half, :] = hpart[c, near, half, :] + hline[0, half, :]
+        summed.append(send(hpart.at[c, near, half, :], hline.at[2, half, :], to_h(near)))
     hidden = acc[links[SLOTS + col]] + hcore[h].astype(F32)
+    for k in range(16, 24):
+        flip[k] = vals[k].T
     plain.wait_recv()
     hidden = hidden + hline[1].astype(F32)
-    summed.wait_recv()
+    for cp in summed:
+        cp.wait_recv()
     hidden = hidden + hline[2].astype(F32)
 
-    for cp in fetched[1:]:
-        cp.wait()
-    pre_act = jnp.dot(hidden, weight[...], precision=HIGHEST, preferred_element_type=F32) + bias[...]
+    pre_act = split_dot(hidden, wsplit[0], wsplit[1]) + bias[...]
     sig = jax.nn.sigmoid(pre_act)
     slope = sig * (1.0 + pre_act * (1.0 - sig))
     grad_pre = (cot[...].astype(F32) * slope).astype(BF16)
     grow[h, c] = grad_pre
 
     own = grow.at[h, c]
-    ahead = send(own, own, to_h(near))
-    behind = send(own, own, to_h(back))
+    aheads = []
+    for half in HALVES:
+        block = grow.at[h, c, half, :]
+        aheads.append(send(block, block, to_h(near)))
     over = [send(own, own, partner)]
     out[...] = (pre_act * sig).astype(BF16)
     stored = [fetch(out, out_to, 5)]
+    behind = send(own, own, to_h(back))
     factor = 1.0 / math.sqrt(TILE * NY * NZ * NX * NH * NC)
     grad_float = grad_pre.astype(F32)
     local = lax.dot_general(hidden, grad_float, (((0,), (0,)), ((), ())), precision=HIGHEST,
@@ -230,9 +254,12 @@
         wbuf[cc, :, :, 0:8, :] = local[:, cols].reshape(NX, NY, 8, TILE)
         wbuf[cc, :, :, 8:16, :] = jnp.broadcast_to(local_bias[:, cols].reshape(1, 1, 1, TILE), (NX, NY, 8, TILE))
     w_core = send(wbuf.at[other_core], wcore, partner)
-    ahead.wait_recv()
+    onward = []
+    for ahead, half in zip(aheads, HALVES):
+        ahead.wait_recv()
+        block = grow.at[back, c, half, :]
+        onward.append(send(block, block, to_h(near)))
     block = grow.at[back, c]
-    onward = send(block, block, to_h(near))
     over.append(send(block, block, partner))
     behind.wait_recv()
     block = grow.at[near, c]
@@ -240,7 +267,8 @@
     w_core.wait_recv()
     wbuf[c] = wbuf[c] + wcore[...]
     w_x = [send(wbuf.at[c, at_x(s)], wx.at[s - 1], to_x(s)) for s in (1, 2, 3)]
-    onward.wait_recv()
+    for cp in onward:
+        cp.wait_recv()
     block = grow.at[far, c]
     over.append(send(block, block, partner))
     for cp in w_x:
@@ -400,8 +428,7 @@
     third_rows = part[y, z, x, THIRD, :].astype(F32) + last_c[0].astype(F32) + last_c[1].astype(F32)
     third_rows = third_rows + last_c[2].astype(F32)
     adjoint = jnp.concatenate([ahead_rows, third_rows], axis=0)
-    gin[...] = lax.dot_general(adjoint, weight[...], (((1,), (1,)), ((), ())), precision=HIGHEST,
-                               preferred_element_type=F32).astype(BF16)
+    gin[...] = split_dot(adjoint, wsplit[2], wsplit[3]).astype(BF16)
     stored.append(fetch(gin, gin_to, 6))
     for cp in copies:
         cp.wait_send()
@@ -445,6 +472,7 @@
         blocks((1, FEAT), F32),
         blocks((TILE, FEAT), BF16),
         blocks((SLOTS, TILE, TILE), BF16),
+        blocks((4, FEAT, FEAT), BF16),
         blocks((NY, NZ, NX, TILE, FEAT), BF16),
         blocks((SLOTS, TILE, TILE), BF16),
         blocks((SLOTS + 1, TILE, FEAT), F32),

time: 135 us -> 134 us (level)
  no operation moved by 1% of the time
where the time goes in v3:
time: 134 us
  Pallas kernels  131 us (98%)
    pallas_call x1, Pallas kernels, per_device(): pl.pallas_call(kernel, out_shape=results, in_specs=[smem, smem] + [anywhe...  130 us

profile of v3, /device:TPU:1, one launch (start us, length us, event | category | flops | bytes accessed | tf_op | source)
XLA Modules:
  0.0 134.2 jit_solution(4951812660431730447)
XLA Ops:
  1.3 0.1 add_minimum_fusion
  1.4 0.0 copy-start
  1.4 0.7 copy-done
  2.1 0.1 broadcast_compare_fusion
  2.2 0.1 select_reduce_fusion
  2.2 0.6 compare_select_fusion.links
  2.8 129.6 %shard_map.102 = (bf16[128,256]{1,0:T(8,128)(2,1)}, f32[256,256]{1,0:T(8,128)}, f32[1,256]{1,0:T(1,128)}, bf16[128,256]{1,0:T(8,128)(2,1)}) custom-call(s32[24]{0:T(128)} %bitcast.10, s32[152]{0:T(256)} %compare_select_fusion.links, bf16[128,256]{1,0:T(8,128)(2,1)} %feat_in.1, f32[256,256]{1,0:T(8,128)} %weight_in.1, f32[1,256]{1,0:T(1,128)} %bitcast.9, ...), custom_call_target="tpu_custom_call" | custom-call | tf_op jit(solution)/shard_map/pallas_call | solution.py:510
  132.4 1.8 %shard_map.103 = (bf16[128,256]{1,0:T(8,128)(2,1)}, f32[256,256]{1,0:T(8,128)}, f32[1,256]{1,0:T(1,128)}, bf16[128,256]{1,0:T(8,128)(2,1)}) custom-call(bf16[128,256]{1,0:T(8,128)(2,1)} %get-tuple-element.12.refs_0_, f32[256,256]{1,0:T(8,128)} %get-tuple-element.13.refs_1_, f32[1,256]{1,0:T(1,128)} %get-tuple-element.14.refs_2_, ...), custom_call_target="tpu_custom_call" | custom-call | tf_op jit(solution)/shard_map/pallas_call | solution.py:519
  (6 shorter events, 0.0 us)
Async XLA Ops:
  1.4 0.7 copy-start
